TPU v7x, 1024 devices: a whole 4x4x32 slice. The times are simulated.
1024 devices in a mesh: ep: 64 (over z, core), fsdp: 16 (over x, y).
Axes of the slice: x: 4, y: 4, z: 32, core: 2. Of those that a mesh axis runs over, the one named last changes fastest.
Arguments:
- tokens: bfloat16 [8192, 3072], P(('ep', 'fsdp')), may hold values from -6 to 6
- out_grad: bfloat16 [8192, 3072], P(('ep', 'fsdp')), may hold values from -6 to 6
- routes: int32 [8192, 2], P(('ep', 'fsdp')), may hold values from 0 to 7, as said below
- probs: bfloat16 [8192, 2], P(('ep', 'fsdp')), may hold values from 0.099609375 to 1
- gate_elems: bfloat16 [3072, 8192], P('fsdp', 'ep'), may hold values from -0.109375 to 0.109375
- gate_scales: bfloat16 [96, 8192], P('fsdp', 'ep'), may hold values from 0.5 to 2
- up_elems: bfloat16 [3072, 8192], P('fsdp', 'ep'), may hold values from -0.109375 to 0.109375
- up_scales: bfloat16 [96, 8192], P('fsdp', 'ep'), may hold values from 0.5 to 2
- down_elems: bfloat16 [8192, 3072], P('ep', 'fsdp'), may hold values from -0.0625 to 0.0625
- down_scales: bfloat16 [8192, 96], P('ep', 'fsdp'), may hold values from 0.5 to 2
Outputs:
- input_grad: bfloat16 [8192, 3072], P(('ep', 'fsdp'))
- prob_grad: float32 [8192], P(('ep', 'fsdp'))
- gate_grad: float32 [3072, 8192], P('fsdp', 'ep')
- up_grad: float32 [3072, 8192], P('fsdp', 'ep')
- down_grad: float32 [8192, 3072], P('ep', 'fsdp')
Inputs may be any that keep to these rules, and one draw needn't show every extreme that they name: `routes`: each token names 2 different experts. Among the 8 tokens of one device, between 1 and 2 name expert 0, and some device has exactly 2.
All inputs are finite; a program needn't handle non-finite values.
Results may differ from a plain program's by a relative error of at most 0.015.
Values may be sent and summed in bfloat16 or wider, within the bound.
No kernel may reach another device: no remote copies, remote signals or barrier semaphores. Data moves between devices by JAX's collectives and lax.ppermute only.
A program may use at most 32 MiB of HBM per device.

v0:
```python
import jax
import jax.numpy as jnp
from jax import lax
from jax.sharding import PartitionSpec as P

BLOCK = 32
CAP = 2


def dequantize(elements, scales, along):
    wide = jnp.repeat(scales.astype(jnp.float32), BLOCK, axis=along)
    return (elements.astype(jnp.float32) * wide).astype(jnp.bfloat16)


def local(
    tokens,
    out_grad,
    routes,
    probs,
    gate_elems,
    gate_scales,
    up_elems,
    up_scales,
    down_elems,
    down_scales,
):
    first = routes[:, 0] == 0
    second = routes[:, 1] == 0
    chosen = jnp.logical_or(first, second)
    weight = jnp.where(
        first, probs[:, 0], jnp.where(second, probs[:, 1], jnp.zeros_like(probs[:, 0]))
    )
    slot = jnp.cumsum(chosen.astype(jnp.int32)) - 1
    slot_ids = jnp.arange(CAP, dtype=jnp.int32)
    select_mask = jnp.logical_and(slot[None, :] == slot_ids[:, None], chosen[None, :])
    select = select_mask.astype(jnp.bfloat16)
    token_buf = jnp.dot(select, tokens, preferred_element_type=jnp.float32).astype(jnp.bfloat16)
    grad_buf = jnp.dot(select, out_grad, preferred_element_type=jnp.float32).astype(jnp.bfloat16)
    weight_buf = jnp.sum(
        select_mask.astype(jnp.float32) * weight.astype(jnp.float32)[None, :], axis=1
    ).astype(jnp.bfloat16)
    rows, grads_rows, weights_rows = (
        lax.all_gather(token_buf, "ep", axis=0, tiled=True),
        lax.all_gather(grad_buf, "ep", axis=0, tiled=True),
        lax.all_gather(weight_buf, "ep", axis=0, tiled=True),
    )
    gate_all, up_all, gate_scale_all, up_scale_all = (
        lax.all_gather(gate_elems, "fsdp", axis=0, tiled=True),
        lax.all_gather(up_elems, "fsdp", axis=0, tiled=True),
        lax.all_gather(gate_scales, "fsdp", axis=0, tiled=True),
        lax.all_gather(up_scales, "fsdp", axis=0, tiled=True),
    )
    down_all, down_scale_all = (
        lax.all_gather(down_elems, "fsdp", axis=1, tiled=True),
        lax.all_gather(down_scales, "fsdp", axis=1, tiled=True),
    )
    w_gate = dequantize(gate_all, gate_scale_all, 0)
    w_up = dequantize(up_all, up_scale_all, 0)
    w_down = dequantize(down_all, down_scale_all, 1)
    hidden_units = w_gate.shape[1]
    row_weights = weights_rows.astype(jnp.float32)
    gate_pre = jnp.dot(rows, w_gate, preferred_element_type=jnp.float32)
    lift_pre = jnp.dot(rows, w_up, preferred_element_type=jnp.float32)
    sigmoid_gate = jax.nn.sigmoid(gate_pre)
    activated = gate_pre * sigmoid_gate
    hidden = (activated * lift_pre).astype(jnp.bfloat16)
    scaled_hidden = (row_weights[:, None] * activated * lift_pre).astype(jnp.bfloat16)
    back = lax.dot_general(
        grads_rows, w_down, (((1,), (1,)), ((), ())), preferred_element_type=jnp.float32
    )
    prob_part = jnp.sum(hidden.astype(jnp.float32) * back, axis=1)
    hidden_grad = row_weights[:, None] * back
    lift_grad = (hidden_grad * activated).astype(jnp.bfloat16)
    gate_pre_grad = (
        hidden_grad * lift_pre * sigmoid_gate * (1.0 + gate_pre * (1.0 - sigmoid_gate))
    ).astype(jnp.bfloat16)
    input_part = lax.dot_general(
        gate_pre_grad, w_gate, (((1,), (1,)), ((), ())), preferred_element_type=jnp.float32
    )
    input_part = input_part + lax.dot_general(
        lift_grad, w_up, (((1,), (1,)), ((), ())), preferred_element_type=jnp.float32
    )
    input_rows, prob_rows = (
        lax.psum_scatter(input_part, "ep", scatter_dimension=0, tiled=True),
        lax.psum_scatter(prob_part, "ep", scatter_dimension=0, tiled=True),
    )
    mask_float = select_mask.astype(jnp.float32)
    input_grad = jnp.sum(
        mask_float[:, :, None] * input_rows.astype(jnp.bfloat16).astype(jnp.float32)[:, None, :],
        axis=0,
    ).astype(jnp.bfloat16)
    prob_grad = jnp.sum(mask_float * prob_rows[:, None], axis=0)
    term_gate = lax.dot_general(
        rows, gate_pre_grad, (((0,), (0,)), ((), ())), preferred_element_type=jnp.float32
    )
    term_up = lax.dot_general(
        rows, lift_grad, (((0,), (0,)), ((), ())), preferred_element_type=jnp.float32
    )
    term_down = lax.dot_general(
        grads_rows, scaled_hidden, (((0,), (0,)), ((), ())), preferred_element_type=jnp.float32
    )
    share = lax.psum_scatter(
        jnp.concatenate([term_gate, term_up, term_down], axis=1).astype(jnp.bfloat16),
        "fsdp",
        scatter_dimension=0,
        tiled=True,
    ).astype(jnp.float32)
    gate_grad = share[:, :hidden_units]
    up_grad = share[:, hidden_units : 2 * hidden_units]
    down_grad = jnp.transpose(share[:, 2 * hidden_units :])
    return (input_grad, prob_grad, gate_grad, up_grad, down_grad)


def solution(mesh):
    in_specs = (
        P(("ep", "fsdp"), None),
        P(("ep", "fsdp"), None),
        P(("ep", "fsdp"), None),
        P(("ep", "fsdp"), None),
        P("fsdp", "ep"),
        P("fsdp", "ep"),
        P("fsdp", "ep"),
        P("fsdp", "ep"),
        P("ep", "fsdp"),
        P("ep", "fsdp"),
    )
    out_specs = (
        P(("ep", "fsdp"), None),
        P(("ep", "fsdp")),
        P("fsdp", "ep"),
        P("fsdp", "ep"),
        P("ep", "fsdp"),
    )
    return jax.shard_map(local, mesh=mesh, in_specs=in_specs, out_specs=out_specs, check_vma=False)
```

profile of v0, /device:TPU:8, one launch (start us, length us, event | category | flops | bytes accessed | tf_op | source)
XLA Modules:
  0.0 668.4 jit_solution(15640179822464340900)
XLA Ops:
  7.2 0.8 bitcast_or_fusion
  8.0 0.8 or_convert_fusion
  9.1 70.9 %all-gather.2 = bf16[64,2,3072]{2,1,0:T(2,128)(2,1)S(1)} all-gather(bf16[1,2,3072]{2,1,0:T(2,128)(2,1)S(1)} %fusion.1), channel_id=1, replica_groups=mesh['ep'=64,'fsdp'=16] {'ep'}, dimensions={0}, use_global_device_ids=true | all-gather | bytes 798720 | tf_op jit(solution)/shard_map/all_gather | solution.py:43
  80.4 24.3 %all_gather.32 = bf16[3072,128]{1,0:T(8,128)(2,1)S(1)} all-gather(bf16[192,128]{1,0:T(8,128)(2,1)S(1)} %copy-done.3), channel_id=1, replica_groups=mesh['ep'=64,'fsdp'=16] {'fsdp'}, dimensions={0}, use_global_device_ids=true | all-gather | bytes 835584 | tf_op jit(solution)/shard_map/all_gather | solution.py:49
  104.6 21.8 %all-gather.3 = bf16[16,6,128]{2,1,0:T(8,128)(2,1)S(1)} all-gather(bf16[1,6,128]{2,1,0:T(8,128)(2,1)S(1)} %bitcast.63), channel_id=1, replica_groups=mesh['ep'=64,'fsdp'=16] {'fsdp'}, dimensions={0}, use_global_device_ids=true | all-gather | bytes 26112 | tf_op jit(solution)/shard_map/all_gather | solution.py:51
  126.4 22.9 %all_gather.34 = bf16[3072,128]{1,0:T(8,128)(2,1)S(1)} all-gather(bf16[192,128]{1,0:T(8,128)(2,1)S(1)} %copy-done.4), channel_id=1, replica_groups=mesh['ep'=64,'fsdp'=16] {'fsdp'}, dimensions={0}, use_global_device_ids=true | all-gather | bytes 835584 | tf_op jit(solution)/shard_map/all_gather | solution.py:48
  149.4 21.7 %all-gather.4 = bf16[16,6,128]{2,1,0:T(8,128)(2,1)S(1)} all-gather(bf16[1,6,128]{2,1,0:T(8,128)(2,1)S(1)} %bitcast.64), channel_id=1, replica_groups=mesh['ep'=64,'fsdp'=16] {'fsdp'}, dimensions={0}, use_global_device_ids=true | all-gather | bytes 26112 | tf_op jit(solution)/shard_map/all_gather | solution.py:50
  171.3 0.4 fusion.13
  172.8 54.2 %all-gather = bf16[64,2,3072]{2,1,0:T(2,128)(2,1)S(1)} all-gather(bf16[1,2,3072]{2,1,0:T(2,128)(2,1)S(1)} %fusion), channel_id=1, replica_groups=mesh['ep'=64,'fsdp'=16] {'ep'}, dimensions={0}, use_global_device_ids=true | all-gather | bytes 798720 | tf_op jit(solution)/shard_map/all_gather | solution.py:44
  227.3 23.1 %all_gather.29 = bf16[128,3072]{0,1:T(8,128)(2,1)S(1)} all-gather(bf16[128,192]{0,1:T(8,128)(2,1)S(1)} %copy-done.5), channel_id=1, replica_groups=mesh['ep'=64,'fsdp'=16] {'fsdp'}, dimensions={1}, use_global_device_ids=true | all-gather | bytes 835584 | tf_op jit(solution)/shard_map/all_gather | solution.py:54
  250.4 21.7 %all-gather.1 = bf16[16,6,128]{2,1,0:T(8,128)(2,1)S(1)} all-gather(bf16[1,6,128]{2,1,0:T(8,128)(2,1)S(1)} %bitcast.65), channel_id=1, replica_groups=mesh['ep'=64,'fsdp'=16] {'fsdp'}, dimensions={0}, use_global_device_ids=true | all-gather | bytes 26112 | tf_op jit(solution)/shard_map/all_gather | solution.py:55
  272.3 0.4 multiply_reduce_fusion.1
  272.8 90.3 %all-reduce.2 = f32[128]{0:T(128)S(1)} all-reduce(f32[128]{0:T(128)S(1)} %get-tuple-element.35), channel_id=3, replica_groups=mesh['ep'=64,'fsdp'=16] {'ep'}, use_global_device_ids=true, to_apply=%region_5.6.clone | all-reduce | flops 128 | bytes 1024
  363.1 1.4 fusion.12
  365.2 0.7 select_reduce_fusion
  366.7 90.4 %all-reduce = bf16[128]{0:T(256)(128)(2,1)S(1)} all-reduce(bf16[128]{0:T(256)(128)(2,1)S(1)} %dynamic-update-slice), channel_id=1, replica_groups=mesh['ep'=64,'fsdp'=16] {'ep'}, use_global_device_ids=true, to_apply=%add | all-reduce | flops 128 | bytes 512
  458.5 2.4 copy.27
  461.3 0.7 copy-done.2
  462.5 195.0 %all-reduce.4 = bf16[128,3072]{1,0:T(8,128)(2,1)S(1)} all-reduce(f32[128,3072]{1,0:T(8,128)S(1)} %convolution_add_fusion), channel_id=2, replica_groups=mesh['ep'=64,'fsdp'=16] {'ep'}, use_global_device_ids=true, to_apply=%region_2.3.clone | all-reduce | flops 393216 | bytes 2359296
  657.5 0.7 multiply_reduce_fusion
  658.2 1.0 copy.28
  659.3 0.7 copy.24
  660.1 0.7 copy.25
  660.8 0.7 copy.26
  (56 shorter events, 4.8 us)
Async XLA Ops:
  7.2 1.8 copy-start
  7.2 73.2 %copy-start.3 = (bf16[192,128]{1,0:T(8,128)(2,1)S(1)}, bf16[192,128]{1,0:T(8,128)(2,1)}, u32[]{:S(2)}) copy-start(bf16[192,128]{1,0:T(8,128)(2,1)} %param.16) | copy-start | bytes 147460
  7.2 651.0 %reduce-scatter.4.cloned.1.call-start = ((), (), s32[]{:S(2)}) async-start(), calls=%async_computation.1 | async-start | bytes 2506752
  9.1 95.5 %copy-start.7 = (bf16[6,128]{1,0:T(8,128)(2,1)S(1)}, bf16[6,128]{1,0:T(8,128)(2,1)}, u32[]{:S(2)}) copy-start(bf16[6,128]{1,0:T(8,128)(2,1)} %param.17) | copy-start | bytes 4612
  9.1 117.3 %copy-start.4 = (bf16[192,128]{1,0:T(8,128)(2,1)S(1)}, bf16[192,128]{1,0:T(8,128)(2,1)}, u32[]{:S(2)}) copy-start(bf16[192,128]{1,0:T(8,128)(2,1)} %param.14) | copy-start | bytes 147460
  80.1 69.3 %copy-start.8 = (bf16[6,128]{1,0:T(8,128)(2,1)S(1)}, bf16[6,128]{1,0:T(8,128)(2,1)}, u32[]{:S(2)}) copy-start(bf16[6,128]{1,0:T(8,128)(2,1)} %param.15) | copy-start | bytes 4612
  171.3 0.9 copy-start.1
  171.8 0.9 copy-start.6
  172.7 54.7 %copy-start.5 = (bf16[128,192]{0,1:T(8,128)(2,1)S(1)}, bf16[128,192]{0,1:T(8,128)(2,1)}, u32[]{:S(2)}) copy-start(bf16[128,192]{0,1:T(8,128)(2,1)} %param.18) | copy-start | bytes 147460
  172.8 77.6 %copy-start.9 = (bf16[128,6]{0,1:T(8,128)(2,1)S(1)}, bf16[128,6]{0,1:T(8,128)(2,1)}, u32[]{:S(2)}) copy-start(bf16[128,6]{0,1:T(8,128)(2,1)} %param.19) | copy-start | bytes 4612
  272.1 90.9 %copy-start.10 = (bf16[8,2]{0,1:T(2,128)(2,1)S(1)}, bf16[8,2]{0,1:T(2,128)(2,1)}, u32[]{:S(2)}) copy-start(bf16[8,2]{0,1:T(2,128)(2,1)} %param.13) | copy-start | bytes 100
  272.2 90.9 %copy-start.11 = (s32[8,2]{0,1:T(2,128)S(1)}, s32[8,2]{0,1:T(2,128)}, u32[]{:S(2)}) copy-start(s32[8,2]{0,1:T(2,128)} %param.12) | copy-start | bytes 196
  460.9 1.1 copy-start.2
Sparse Core Ops, SparseCore 0:
  461.1 101.9 reduce-scatter.3
where the time goes:
time: 669 us; the launch traced here: 668 us
  blocking collectives  636 us (95%)
  between operations  15.7 us (2%)
  local copies, waits for them, and re-layouts  9.12 us (1%)
    unnamed x3, blocking collectives  376 us
    all_gather x1, blocking collectives, local(): lax.all_gather(token_buf, 'ep', axis=0, tiled=True)  70.9 us
    all_gather x1, blocking collectives, local(): lax.all_gather(grad_buf, 'ep', axis=0, tiled=True)  54.2 us
    all_gather x1, blocking collectives, local(): lax.all_gather(up_elems, 'fsdp', axis=0, tiled=True)  24.3 us
    all_gather x1, blocking collectives, local(): lax.all_gather(down_elems, 'fsdp', axis=1, tiled=True)  23.1 us
    all_gather x1, blocking collectives, local(): lax.all_gather(gate_elems, 'fsdp', axis=0, tiled=True)  22.9 us
    all_gather x1, blocking collectives, local(): lax.all_gather(up_scales, 'fsdp', axis=0, tiled=True)  21.8 us
    all_gather x1, blocking collectives, local(): lax.all_gather(gate_scales, 'fsdp', axis=0, tiled=True)  21.7 us
  transfers between devices with their start and end apart: 1, of which 0 were waited for; matrix products, arithmetic and copies ran while one was open for 0% of the time, Pallas kernels for 0%

commit v1 on v0

v1 whole, which is shorter than its diff:
```python
import jax
import jax.numpy as jnp
from jax import lax
from jax.sharding import Mesh, PartitionSpec as P

BLOCK = 32
CAP = 2
FAR, NEAR, CORES = 8, 4, 2
X, Y = 4, 4
N_FSDP = X * Y
BF16 = jnp.bfloat16
F32 = jnp.float32


def dequantize(elements, scales):
    groups = elements.shape[0] // BLOCK
    wide = elements.reshape(groups, BLOCK, -1).astype(F32)
    return (wide * scales.astype(F32)[:, None, :]).astype(BF16).reshape(elements.shape)


def local(
    tokens,
    out_grad,
    routes,
    probs,
    gate_elems,
    gate_scales,
    up_elems,
    up_scales,
    down_elems,
    down_scales,
):
    width = tokens.shape[1]
    first = routes[:, 0] == 0
    second = routes[:, 1] == 0
    chosen = jnp.logical_or(first, second)
    weight = jnp.where(
        first, probs[:, 0], jnp.where(second, probs[:, 1], jnp.zeros_like(probs[:, 0]))
    )
    slot = jnp.cumsum(chosen.astype(jnp.int32)) - 1
    slot_ids = jnp.arange(CAP, dtype=jnp.int32)
    select_mask = jnp.logical_and(slot[None, :] == slot_ids[:, None], chosen[None, :])
    select = select_mask.astype(BF16)
    wide_weight = jnp.broadcast_to(weight[:, None], (weight.shape[0], 128))
    both = jnp.concatenate([tokens, out_grad, wide_weight], axis=1)
    payload = jnp.dot(select, both, preferred_element_type=F32).astype(BF16)

    own = jnp.concatenate(
        [
            dequantize(gate_elems, gate_scales),
            dequantize(up_elems, up_scales),
            dequantize(down_elems.T, down_scales.T),
        ],
        axis=1,
    )
    everyone = jnp.broadcast_to(own[None], (N_FSDP,) + own.shape)
    everyone, payload = lax.optimization_barrier((everyone, payload))
    weights = lax.all_to_all(everyone, ("x", "y"), 0, 0, tiled=True)

    along_z = lax.all_gather(payload[None], ("far", "near"), axis=0, tiled=True)
    along_z = along_z.reshape(FAR * NEAR * CAP, payload.shape[1])
    along_z, weights = lax.optimization_barrier((along_z, weights))
    pair = jnp.broadcast_to(along_z[None], (CORES,) + along_z.shape)
    pair = lax.all_to_all(pair, "core", 0, 0, tiled=True)
    all_rows = pair.reshape(CORES * FAR * NEAR * CAP, payload.shape[1])
    rows = all_rows[:, :width]
    grads_rows = all_rows[:, width : 2 * width]
    row_weights = all_rows[:, 2 * width : 2 * width + 1].astype(F32)

    weights = weights.reshape(N_FSDP * own.shape[0], own.shape[1])
    units = gate_elems.shape[1]
    w_gate, w_up, w_down = (
        weights[:, :units],
        weights[:, units : 2 * units],
        weights[:, 2 * units :],
    )

    gate_pre = jnp.dot(rows, w_gate, preferred_element_type=F32)
    lift_pre = jnp.dot(rows, w_up, preferred_element_type=F32)
    back = jnp.dot(grads_rows, w_down, preferred_element_type=F32)
    sigmoid_gate = jax.nn.sigmoid(gate_pre)
    activated = gate_pre * sigmoid_gate
    hidden = (activated * lift_pre).astype(BF16)
    scaled_hidden = (row_weights * activated * lift_pre).astype(BF16)
    prob_part = jnp.sum(hidden.astype(F32) * back, axis=1, keepdims=True)
    hidden_grad = row_weights * back
    lift_grad = (hidden_grad * activated).astype(BF16)
    gate_pre_grad = (
        hidden_grad * lift_pre * sigmoid_gate * (1.0 + gate_pre * (1.0 - sigmoid_gate))
    ).astype(BF16)

    def over_rows(a, b):
        return lax.dot_general(a, b, (((0,), (0,)), ((), ())), preferred_element_type=F32)

    terms = jnp.concatenate(
        [
            over_rows(rows, gate_pre_grad),
            over_rows(rows, lift_grad),
            over_rows(grads_rows, scaled_hidden),
        ],
        axis=1,
    ).astype(BF16)
    terms = terms.reshape((N_FSDP,) + own.shape)
    input_part = lax.dot_general(
        jnp.concatenate([gate_pre_grad, lift_grad], axis=1),
        weights[:, : 2 * units],
        (((1,), (1,)), ((), ())),
        preferred_element_type=F32,
    )

    def pack(values, prob):
        high = prob.astype(BF16)
        low = (prob - high.astype(F32)).astype(BF16)
        pad = jnp.zeros(prob.shape[:-1] + (126,), BF16)
        return jnp.concatenate([values.astype(BF16), high, low, pad], axis=-1)

    def unpack(blocks):
        total = jnp.sum(blocks.astype(F32), axis=0)
        prob = total[..., width : width + 1] + total[..., width + 1 : width + 2]
        return total[..., :width], prob

    part = pack(input_part, prob_part).reshape(CORES, FAR * NEAR * CAP, -1)
    part = lax.all_to_all(part, "core", 0, 0, tiled=True)
    part = pack(*unpack(part)).reshape(FAR, NEAR, CAP, -1)
    part = jnp.swapaxes(part, 0, 1).reshape(NEAR, FAR * CAP, -1)
    part = lax.all_to_all(part, "near", 0, 0, tiled=True)
    part = pack(*unpack(part))
    part, terms = lax.optimization_barrier((part, terms))
    shares = lax.all_to_all(terms, ("x", "y"), 0, 0, tiled=True)
    share = jnp.sum(shares.astype(F32), axis=0)
    part = lax.all_gather(part[None], "far", axis=0, tiled=True)
    mine = CAP * lax.axis_index("far")
    input_rows, prob_rows = unpack(lax.dynamic_slice_in_dim(part, mine, CAP, axis=1))

    mask_float = select_mask.astype(F32)
    input_grad = jnp.sum(
        mask_float[:, :, None] * input_rows.astype(BF16).astype(F32)[:, None, :], axis=0
    ).astype(BF16)
    prob_grad = jnp.sum(mask_float * prob_rows, axis=0)
    gate_grad = share[:, :units]
    up_grad = share[:, units : 2 * units]
    down_grad = share[:, 2 * units :].T
    return (input_grad, prob_grad, gate_grad, up_grad, down_grad)


def solution(mesh):
    fine = Mesh(
        mesh.devices.reshape(FAR, NEAR, CORES, X, Y), ("far", "near", "core", "x", "y")
    )
    ep, fsdp = ("far", "near", "core"), ("x", "y")
    by_token = P(ep + fsdp, None)
    tall, wide = P(fsdp, ep), P(ep, fsdp)
    in_specs = (by_token,) * 4 + (tall,) * 4 + (wide,) * 2
    out_specs = (by_token, P(ep + fsdp), tall, tall, wide)
    return jax.shard_map(
        local, mesh=fine, in_specs=in_specs, out_specs=out_specs, check_vma=False
    )
```

time: 669 us -> 190 us (0.28)
  the two profiles are of different devices: /device:TPU:8 before, /device:TPU:2 now
where the time goes in v1:
time: 190 us; the launch traced here: 189 us
  blocking collectives  127 us (67%)
  starting transfers between devices  27.5 us (14%)
  waiting for transfers between devices  9.6 us (5%)
  other arithmetic  9.47 us (5%)
  local copies, waits for them, and re-layouts  8.9 us (5%)
  matrix products  5.53 us (3%)
    all_gather x1, blocking collectives, local(): along_z = lax.all_gather(payload[None], ('far', 'near'), axis=0, tiled=True)  68.1 us
    all_gather x1, blocking collectives, local(): part = lax.all_gather(part[None], 'far', axis=0, tiled=True)  49.7 us
    all_to_all x1, starting transfers between devices, local(): weights = lax.all_to_all(everyone, ('x', 'y'), 0, 0, tiled=True)  16.7 us
    all_to_all x1, waiting for transfers between devices, local(): part = lax.all_to_all(part, 'near', 0, 0, tiled=True)  9.6 us
    all_to_all x1, starting transfers between devices, local(): shares = lax.all_to_all(terms, ('x', 'y'), 0, 0, tiled=True)  7.35 us
    all_to_all x1, blocking collectives, local(): pair = lax.all_to_all(pair, 'core', 0, 0, tiled=True)  5.14 us
    all_to_all x1, blocking collectives, local(): part = lax.all_to_all(part, 'core', 0, 0, tiled=True)  4.37 us
  transfers between devices with their start and end apart: 3, of which 1 were waited for; matrix products, arithmetic and copies ran while one was open for 4% of the time, Pallas kernels for 0%

profile of v1, /device:TPU:2, one launch (start us, length us, event | category | flops | bytes accessed | tf_op | source)
XLA Modules:
  0.0 189.2 jit_solution(536460777703825975)
XLA Ops:
  0.6 0.7 convert_bitcast_fusion
  1.3 0.7 convert_element_type.161
  2.0 0.7 convert_element_type.158
  2.7 0.8 fusion.35
  3.4 0.8 fusion.29
  4.4 0.8 fusion.20
  5.2 0.8 fusion.18
  6.2 1.0 convolution_convert_fusion
  7.1 1.7 broadcast_in_dim.18
  8.9 16.7 %all-to-all-start = ((bf16[16,192,384]{2,1,0:T(8,128)(2,1)}), bf16[16,192,384]{2,1,0:T(8,128)(2,1)S(1)}, u32[]{:S(2)}, u32[]{:S(2)}) async-start(bf16[16,192,384]{2,1,0:T(8,128)(2,1)} %broadcast_in_dim.18), calls=%async_computation | async-start | bytes 4718592 | tf_op jit(solution)/shard_map/all_to_all | solution.py:58
  25.6 68.1 %all-gather.2 = bf16[32,2,6272]{2,1,0:T(2,128)(2,1)} all-gather(bf16[1,2,6272]{2,1,0:T(2,128)(2,1)S(1)} %bitcast.53), channel_id=2, replica_groups=mesh['far'=8,'near'=4,'core'=2,'x'=4,'y'=4] {'far','near'}, dimensions={0}, use_global_device_ids=true | all-gather | bytes 827904 | tf_op jit(solution)/shard_map/all_gather | solution.py:60
  93.7 2.3 %reshape.168 = bf16[64,6272]{1,0:T(8,128)(2,1)S(1)} reshape(bf16[32,2,6272]{2,1,0:T(2,128)(2,1)} %all-gather.2) | data formatting | bytes 1605632 | tf_op jit(solution)/shard_map/optimization_barrier | solution.py:62
  96.0 1.4 copy-done
  97.6 5.1 %all_to_all.25 = bf16[2,64,6272]{2,1,0:T(8,128)(2,1)S(1)} all-to-all(bf16[2,64,6272]{2,1,0:T(8,128)(2,1)S(1)} %broadcast_in_dim.22), channel_id=1, replica_groups=mesh['far'=8,'near'=4,'core'=2,'x'=4,'y'=4] {'core'}, dimensions={0} | all-to-all | bytes 3211264 | tf_op jit(solution)/shard_map/all_to_all | solution.py:64
  104.5 2.1 %convolution_convert_fusion.4 = bf16[128,3072]{1,0:T(8,128)(2,1)S(1)} fusion(bf16[3072,384]{1,0:T(8,128)(2,1)} %bitcast.42, bf16[128,128]{0,1:T(8,128)(2,1)S(1)} %get-tuple-element.30, bf16[128,128]{0,1:T(8,128)(2,1)S(1)} %get-tuple-element.29), kind=kOutput, calls=%fused_computation.5 | convolution fusion | flops 201850880 | bytes 2424832 | tf_op jit(solution)/shard_map/dot_general | solution.py:104
  106.9 4.4 %all_to_all.26 = bf16[2,64,3200]{2,1,0:T(8,128)(2,1)S(1)} all-to-all(bf16[2,64,3200]{2,1,0:T(8,128)(2,1)S(1)} %concatenate.36), channel_id=1, replica_groups=mesh['far'=8,'near'=4,'core'=2,'x'=4,'y'=4] {'core'}, dimensions={0} | all-to-all | bytes 1638400 | tf_op jit(solution)/shard_map/all_to_all | solution.py:123
  112.3 0.8 copy.53
  113.1 3.5 %all-to-all-start.3 = ((bf16[4,16,3200]{2,1,0:T(8,128)(2,1)}), bf16[4,16,3200]{2,1,0:T(8,128)(2,1)S(1)}, u32[]{:S(2)}, u32[]{:S(2)}) async-start(bf16[4,16,3200]{2,1,0:T(8,128)(2,1)} %copy.53), calls=%async_computation.3 | async-start | bytes 819200 | tf_op jit(solution)/shard_map/all_to_all | solution.py:126
  117.8 1.8 pad_maximum_fusion
  119.6 9.6 %all-to-all-done.3 = bf16[4,16,3200]{2,1,0:T(8,128)(2,1)S(1)} async-done(((bf16[4,16,3200]{2,1,0:T(8,128)(2,1)}), bf16[4,16,3200]{2,1,0:T(8,128)(2,1)S(1)}, u32[]{:S(2)}, u32[]{:S(2)}) %all-to-all-start.3) | async-done | bytes 409632 | tf_op jit(solution)/shard_map/all_to_all | solution.py:126
  129.4 7.3 %all-to-all-start.4 = ((bf16[16,192,384]{2,1,0:T(8,128)(2,1)}), bf16[16,192,384]{2,1,0:T(8,128)(2,1)S(1)}, u32[]{:S(2)}, u32[]{:S(2)}) async-start(bf16[16,192,384]{2,1,0:T(8,128)(2,1)} %pad_maximum_fusion), calls=%async_computation.4 | async-start | bytes 4718592 | tf_op jit(solution)/shard_map/all_to_all | solution.py:129
  136.8 49.7 %all-gather.1 = bf16[128,3200]{1,0:T(8,128)(2,1)S(1)} all-gather(bf16[16,3200]{1,0:T(8,128)(2,1)S(1)} %concatenate.38), channel_id=3, replica_groups=mesh['far'=8,'near'=4,'core'=2,'x'=4,'y'=4] {'far'}, dimensions={0}, use_global_device_ids=true | all-gather | bytes 921600 | tf_op jit(solution)/shard_map/all_gather | solution.py:131
  187.5 0.7 multiply_reduce_fusion
  188.5 0.7 slice_bitcast_fusion
  (47 shorter events, 6.2 us)
Async XLA Ops:
  8.9 87.2 %all-to-all-start = ((bf16[16,192,384]{2,1,0:T(8,128)(2,1)}), bf16[16,192,384]{2,1,0:T(8,128)(2,1)S(1)}, u32[]{:S(2)}, u32[]{:S(2)}) async-start(bf16[16,192,384]{2,1,0:T(8,128)(2,1)} %broadcast_in_dim.18), calls=%async_computation | async-start | bytes 4718592 | tf_op jit(solution)/shard_map/all_to_all | solution.py:58
  96.0 1.4 copy-start
  97.6 5.1 %copy-start.1 = (bf16[16,192,384]{2,1,0:T(8,128)(2,1)S(1)}, bf16[16,192,384]{2,1,0:T(8,128)(2,1)}, u32[]{:S(2)}) copy-start(bf16[16,192,384]{2,1,0:T(8,128)(2,1)} %copy-done) | copy-start | bytes 7077892
  113.1 16.0 %all-to-all-start.3 = ((bf16[4,16,3200]{2,1,0:T(8,128)(2,1)}), bf16[4,16,3200]{2,1,0:T(8,128)(2,1)S(1)}, u32[]{:S(2)}, u32[]{:S(2)}) async-start(bf16[4,16,3200]{2,1,0:T(8,128)(2,1)} %copy.53), calls=%async_computation.3 | async-start | bytes 819200 | tf_op jit(solution)/shard_map/all_to_all | solution.py:126
  129.4 58.8 %all-to-all-start.4 = ((bf16[16,192,384]{2,1,0:T(8,128)(2,1)}), bf16[16,192,384]{2,1,0:T(8,128)(2,1)S(1)}, u32[]{:S(2)}, u32[]{:S(2)}) async-start(bf16[16,192,384]{2,1,0:T(8,128)(2,1)} %pad_maximum_fusion), calls=%async_computation.4 | async-start | bytes 4718592 | tf_op jit(solution)/shard_map/all_to_all | solution.py:129

commit v2 on v1

--- a/solution.py
+++ b/solution.py
@@ -6,6 +6,8 @@
 BLOCK = 32
 CAP = 2
 FAR, NEAR, CORES = 8, 4, 2
+FAR_AXES, NEAR_AXES = ("za", "zb"), ("zc", "zd")
+SWAP = [(0, 1), (1, 0)]
 X, Y = 4, 4
 N_FSDP = X * Y
 BF16 = jnp.bfloat16
@@ -57,8 +59,9 @@
     everyone, payload = lax.optimization_barrier((everyone, payload))
     weights = lax.all_to_all(everyone, ("x", "y"), 0, 0, tiled=True)
 
-    along_z = lax.all_gather(payload[None], ("far", "near"), axis=0, tiled=True)
-    along_z = along_z.reshape(FAR * NEAR * CAP, payload.shape[1])
+    along_z = lax.all_gather(payload[None], FAR_AXES, axis=0, tiled=True)
+    along_z = along_z.reshape(FAR * CAP, payload.shape[1])
+    along_z = lax.all_gather(along_z, NEAR_AXES, axis=0, tiled=True)
     along_z, weights = lax.optimization_barrier((along_z, weights))
     pair = jnp.broadcast_to(along_z[None], (CORES,) + along_z.shape)
     pair = lax.all_to_all(pair, "core", 0, 0, tiled=True)
@@ -121,15 +124,22 @@
 
     part = pack(input_part, prob_part).reshape(CORES, FAR * NEAR * CAP, -1)
     part = lax.all_to_all(part, "core", 0, 0, tiled=True)
-    part = pack(*unpack(part)).reshape(FAR, NEAR, CAP, -1)
-    part = jnp.swapaxes(part, 0, 1).reshape(NEAR, FAR * CAP, -1)
-    part = lax.all_to_all(part, "near", 0, 0, tiled=True)
+    part = pack(*unpack(part)).reshape(NEAR, FAR * CAP, -1)
+    part = lax.all_to_all(part, NEAR_AXES, 0, 0, tiled=True)
     part = pack(*unpack(part))
     part, terms = lax.optimization_barrier((part, terms))
     shares = lax.all_to_all(terms, ("x", "y"), 0, 0, tiled=True)
     share = jnp.sum(shares.astype(F32), axis=0)
-    part = lax.all_gather(part[None], "far", axis=0, tiled=True)
-    mine = CAP * lax.axis_index("far")
+
+    def halve(part, axis, where):
+        bit = lax.axis_index(axis)
+        keep = lax.dynamic_index_in_dim(part, bit, where, keepdims=False)
+        give = lax.dynamic_index_in_dim(part, 1 - bit, where, keepdims=False)
+        return pack(*unpack(jnp.stack([keep, lax.ppermute(give, axis, SWAP)])))
+
+    part = halve(part.reshape(4, 2, CAP, -1), "zb", 1).reshape(4 * CAP, -1)
+    part = lax.all_gather(part[None], "za", axis=0, tiled=True)
+    mine = CAP * lax.axis_index("za")
     input_rows, prob_rows = unpack(lax.dynamic_slice_in_dim(part, mine, CAP, axis=1))
 
     mask_float = select_mask.astype(F32)
@@ -145,9 +155,10 @@
 
 def solution(mesh):
     fine = Mesh(
-        mesh.devices.reshape(FAR, NEAR, CORES, X, Y), ("far", "near", "core", "x", "y")
+        mesh.devices.reshape(4, 2, 2, 2, CORES, X, Y),
+        FAR_AXES + NEAR_AXES + ("core", "x", "y"),
     )
-    ep, fsdp = ("far", "near", "core"), ("x", "y")
+    ep, fsdp = FAR_AXES + NEAR_AXES + ("core",), ("x", "y")
     by_token = P(ep + fsdp, None)
     tall, wide = P(fsdp, ep), P(ep, fsdp)
     in_specs = (by_token,) * 4 + (tall,) * 4 + (wide,) * 2

time: 190 us -> 170 us (0.89)
  the two profiles are of different devices: /device:TPU:2 before, /device:TPU:14 now
where the time goes in v2:
time: 170 us; the launch traced here: 169 us
  blocking collectives  99.2 us (58%)
  starting transfers between devices  32 us (19%)
  waiting for transfers between devices  15.6 us (9%)
  other arithmetic  9.61 us (6%)
  local copies, waits for them, and re-layouts  6.55 us (4%)
  matrix products  5.53 us (3%)
    all_gather x1, blocking collectives, local(): along_z = lax.all_gather(payload[None], FAR_AXES, axis=0, tiled=True)  43.4 us
    all_gather x1, blocking collectives, local(): part = lax.all_gather(part[None], 'za', axis=0, tiled=True)  29.8 us
    all_to_all x1, starting transfers between devices, local(): weights = lax.all_to_all(everyone, ('x', 'y'), 0, 0, tiled=True)  16.6 us
    all_gather x1, blocking collectives, local(): along_z = lax.all_gather(along_z, NEAR_AXES, axis=0, tiled=True)  16.6 us
    all_to_all x1, waiting for transfers between devices, local(): part = lax.all_to_all(part, NEAR_AXES, 0, 0, tiled=True)  9.6 us
    all_to_all x1, starting transfers between devices, local(): shares = lax.all_to_all(terms, ('x', 'y'), 0, 0, tiled=True)  7.78 us
    ppermute x1, waiting for transfers between devices, halve(): return pack(*unpack(jnp.stack([keep, lax.ppermute(give, axis, SWAP)])))  5.98 us
    all_to_all x1, blocking collectives, local(): pair = lax.all_to_all(pair, 'core', 0, 0, tiled=True)  5.14 us
  transfers between devices with their start and end apart: 4, of which 2 were waited for; matrix products, arithmetic and copies ran while one was open for 3% of the time, Pallas kernels for 0%

profile of v2, /device:TPU:14, one launch (start us, length us, event | category | flops | bytes accessed | tf_op | source)
XLA Modules:
  0.0 169.5 jit_solution(1026696257549614329)
XLA Ops:
  0.6 0.7 convert_bitcast_fusion
  2.7 0.8 fusion.37
  3.4 0.8 fusion.30
  4.4 0.8 fusion.20
  5.2 0.8 fusion.18
  6.2 1.0 convolution_convert_fusion
  7.1 1.7 %broadcast_in_dim.18 = bf16[16,192,384]{2,1,0:T(8,128)(2,1)} broadcast(bf16[192,384]{1,0:T(8,128)(2,1)S(1)} %pad_maximum_fusion.1), dimensions={1,2} | broadcast | bytes 2506752 | tf_op jit(solution)/shard_map/broadcast_in_dim | solution.py:58
  8.9 16.6 %all-to-all-start = ((bf16[16,192,384]{2,1,0:T(8,128)(2,1)}), bf16[16,192,384]{2,1,0:T(8,128)(2,1)S(1)}, u32[]{:S(2)}, u32[]{:S(2)}) async-start(bf16[16,192,384]{2,1,0:T(8,128)(2,1)} %broadcast_in_dim.18), calls=%async_computation | async-start | bytes 4718592 | tf_op jit(solution)/shard_map/all_to_all | solution.py:60
  25.5 43.4 %all-gather.1 = bf16[8,2,6272]{2,1,0:T(2,128)(2,1)S(1)} all-gather(bf16[1,2,6272]{2,1,0:T(2,128)(2,1)S(1)} %bitcast.58), channel_id=2, replica_groups=mesh['za'=4,'zb'=2,'zc'=2,'zd'=2,'core'=2,'x'=4,'y'=4] {'za','zb'}, dimensions={0}, use_global_device_ids=true | all-gather | bytes 225792 | tf_op jit(solution)/shard_map/all_gather | solution.py:62
  69.0 16.6 %all_gather.10 = bf16[64,6272]{1,0:T(8,128)(2,1)S(1)} all-gather(bf16[16,6272]{1,0:T(8,128)(2,1)S(1)} %reshape.168), channel_id=1, replica_groups=mesh['za'=4,'zb'=2,'zc'=2,'zd'=2,'core'=2,'x'=4,'y'=4] {'zc','zd'}, dimensions={0}, use_global_device_ids=true | all-gather | bytes 1003520 | tf_op jit(solution)/shard_map/all_gather | solution.py:64
  85.5 1.4 copy-done
  87.1 5.1 %all_to_all.25 = bf16[2,64,6272]{2,1,0:T(8,128)(2,1)S(1)} all-to-all(bf16[2,64,6272]{2,1,0:T(8,128)(2,1)S(1)} %broadcast_in_dim.22), channel_id=1, replica_groups=mesh['za'=4,'zb'=2,'zc'=2,'zd'=2,'core'=2,'x'=4,'y'=4] {'core'}, dimensions={0} | all-to-all | bytes 3211264 | tf_op jit(solution)/shard_map/all_to_all | solution.py:67
  94.0 2.1 %convolution_convert_fusion.4 = bf16[128,3072]{1,0:T(8,128)(2,1)S(1)} fusion(bf16[3072,384]{1,0:T(8,128)(2,1)} %bitcast.47, bf16[128,128]{0,1:T(8,128)(2,1)S(1)} %get-tuple-element.32, bf16[128,128]{0,1:T(8,128)(2,1)S(1)} %get-tuple-element.31), kind=kOutput, calls=%fused_computation.5 | convolution fusion | flops 201850880 | bytes 2424832 | tf_op jit(solution)/shard_map/dot_general | solution.py:107
  96.4 4.4 %all_to_all.26 = bf16[2,64,3200]{2,1,0:T(8,128)(2,1)S(1)} all-to-all(bf16[2,64,3200]{2,1,0:T(8,128)(2,1)S(1)} %concatenate.39), channel_id=1, replica_groups=mesh['za'=4,'zb'=2,'zc'=2,'zd'=2,'core'=2,'x'=4,'y'=4] {'core'}, dimensions={0} | all-to-all | bytes 1638400 | tf_op jit(solution)/shard_map/all_to_all | solution.py:126
  101.4 0.9 concatenate.40
  102.2 3.5 %all-to-all-start.3 = ((bf16[4,16,3200]{2,1,0:T(8,128)(2,1)}), bf16[4,16,3200]{2,1,0:T(8,128)(2,1)S(1)}, u32[]{:S(2)}, u32[]{:S(2)}) async-start(bf16[4,16,3200]{2,1,0:T(8,128)(2,1)} %bitcast.12), calls=%async_computation.3 | async-start | bytes 819200 | tf_op jit(solution)/shard_map/all_to_all | solution.py:128
  106.9 1.8 %pad_maximum_fusion = bf16[16,192,384]{2,1,0:T(8,128)(2,1)} fusion(bf16[16,192,128]{2,1,0:T(8,128)(2,1)S(1)} %bitcast.53, bf16[16,192,128]{2,1,0:T(8,128)(2,1)S(1)} %bitcast.51, bf16[16,192,128]{2,1,0:T(8,128)(2,1)S(1)} %bitcast.52), kind=kLoop, calls=%fused_computation.6 | loop fusion | flops 7077888 | bytes 4718592 | tf_op jit(solution)/shard_map/concatenate | solution.py:98
  108.7 9.6 %all-to-all-done.3 = bf16[4,16,3200]{2,1,0:T(8,128)(2,1)S(1)} async-done(((bf16[4,16,3200]{2,1,0:T(8,128)(2,1)}), bf16[4,16,3200]{2,1,0:T(8,128)(2,1)S(1)}, u32[]{:S(2)}, u32[]{:S(2)}) %all-to-all-start.3) | async-done | bytes 409632 | tf_op jit(solution)/shard_map/all_to_all | solution.py:128
  118.5 7.8 %all-to-all-start.4 = ((bf16[16,192,384]{2,1,0:T(8,128)(2,1)}), bf16[16,192,384]{2,1,0:T(8,128)(2,1)S(1)}, u32[]{:S(2)}, u32[]{:S(2)}) async-start(bf16[16,192,384]{2,1,0:T(8,128)(2,1)} %pad_maximum_fusion), calls=%async_computation.4 | async-start | bytes 4718592 | tf_op jit(solution)/shard_map/all_to_all | solution.py:131
  126.5 4.2 %collective-permute-start = (bf16[4,2,3200]{2,0,1:T(4,128)(2,1)S(1)}, bf16[4,2,3200]{2,0,1:T(4,128)(2,1)S(1)}, u32[]{:S(2)}, u32[]{:S(2)}) collective-permute-start(bf16[4,2,3200]{2,0,1:T(4,128)(2,1)S(1)} %bitcast.56), channel_id=1, source_target_pairs={{0,128},{128,0},{1,129},{129,1},{2,130},{130,2},{3,131},{131,3},{4... | collective-permute-start | bytes 153608 | tf_op jit(solution)/shard_map/ppermute | solution.py:138
  130.7 6.0 %collective-permute-done = bf16[4,2,3200]{2,0,1:T(4,128)(2,1)S(1)} collective-permute-done((bf16[4,2,3200]{2,0,1:T(4,128)(2,1)S(1)}, bf16[4,2,3200]{2,0,1:T(4,128)(2,1)S(1)}, u32[]{:S(2)}, u32[]{:S(2)}) %collective-permute-start) | collective-permute-done | bytes 51232 | tf_op jit(solution)/shard_map/ppermute | solution.py:138
  137.1 29.8 %all_gather.11 = bf16[4,8,3200]{2,1,0:T(8,128)(2,1)S(1)} all-gather(bf16[1,8,3200]{2,1,0:T(8,128)(2,1)S(1)} %broadcast_in_dim_reshape.3), channel_id=1, replica_groups=mesh['za'=4,'zb'=2,'zc'=2,'zd'=2,'core'=2,'x'=4,'y'=4] {'za'}, dimensions={0}, use_global_device_ids=true | all-gather | bytes 256000 | tf_op jit(solution)/shard_map/all_gather | solution.py:141
  167.7 0.7 multiply_reduce_fusion
  168.7 0.7 slice_bitcast_fusion
  (57 shorter events, 7.6 us)
Async XLA Ops:
  8.9 76.7 %all-to-all-start = ((bf16[16,192,384]{2,1,0:T(8,128)(2,1)}), bf16[16,192,384]{2,1,0:T(8,128)(2,1)S(1)}, u32[]{:S(2)}, u32[]{:S(2)}) async-start(bf16[16,192,384]{2,1,0:T(8,128)(2,1)} %broadcast_in_dim.18), calls=%async_computation | async-start | bytes 4718592 | tf_op jit(solution)/shard_map/all_to_all | solution.py:60
  85.5 1.4 copy-start
  87.1 5.1 %copy-start.1 = (bf16[16,192,384]{2,1,0:T(8,128)(2,1)S(1)}, bf16[16,192,384]{2,1,0:T(8,128)(2,1)}, u32[]{:S(2)}) copy-start(bf16[16,192,384]{2,1,0:T(8,128)(2,1)} %copy-done) | copy-start | bytes 7077892
  102.2 16.0 %all-to-all-start.3 = ((bf16[4,16,3200]{2,1,0:T(8,128)(2,1)}), bf16[4,16,3200]{2,1,0:T(8,128)(2,1)S(1)}, u32[]{:S(2)}, u32[]{:S(2)}) async-start(bf16[4,16,3200]{2,1,0:T(8,128)(2,1)} %bitcast.12), calls=%async_computation.3 | async-start | bytes 819200 | tf_op jit(solution)/shard_map/all_to_all | solution.py:128
  118.5 49.9 %all-to-all-start.4 = ((bf16[16,192,384]{2,1,0:T(8,128)(2,1)}), bf16[16,192,384]{2,1,0:T(8,128)(2,1)S(1)}, u32[]{:S(2)}, u32[]{:S(2)}) async-start(bf16[16,192,384]{2,1,0:T(8,128)(2,1)} %pad_maximum_fusion), calls=%async_computation.4 | async-start | bytes 4718592 | tf_op jit(solution)/shard_map/all_to_all | solution.py:131
  126.5 10.2 %collective-permute-start = (bf16[4,2,3200]{2,0,1:T(4,128)(2,1)S(1)}, bf16[4,2,3200]{2,0,1:T(4,128)(2,1)S(1)}, u32[]{:S(2)}, u32[]{:S(2)}) collective-permute-start(bf16[4,2,3200]{2,0,1:T(4,128)(2,1)S(1)} %bitcast.56), channel_id=1, source_target_pairs={{0,128},{128,0},{1,129},{129,1},{2,130},{130,2},{3,131},{131,3},{4... | collective-permute-start | bytes 153608 | tf_op jit(solution)/shard_map/ppermute | solution.py:138

commit v3 on v2

--- a/solution.py
+++ b/solution.py
@@ -1,6 +1,8 @@
 import jax
 import jax.numpy as jnp
 from jax import lax
+from jax.experimental import pallas as pl
+from jax.experimental.pallas import tpu as pltpu
 from jax.sharding import Mesh, PartitionSpec as P
 
 BLOCK = 32
@@ -14,10 +16,60 @@
 F32 = jnp.float32
 
 
-def dequantize(elements, scales):
-    groups = elements.shape[0] // BLOCK
-    wide = elements.reshape(groups, BLOCK, -1).astype(F32)
-    return (wide * scales.astype(F32)[:, None, :]).astype(BF16).reshape(elements.shape)
+def prepare(
+    tokens,
+    out_grad,
+    routes,
+    probs,
+    gate_elems,
+    gate_scales,
+    up_elems,
+    up_scales,
+    down_elems,
+    down_scales,
+    payload,
+    everyone,
+):
+    width = tokens.shape[1]
+    weights = (
+        (gate_elems, gate_scales),
+        (up_elems, up_scales),
+        (down_elems, down_scales),
+    )
+    for place, (elements, scales) in enumerate(weights):
+        units = elements.shape[1]
+        columns = slice(place * units, (place + 1) * units)
+        wide = scales[...].astype(F32)
+        for group in range(scales.shape[0]):
+            rows = slice(group * BLOCK, (group + 1) * BLOCK)
+            scaled = (elements[rows, :].astype(F32) * wide[group : group + 1, :]).astype(BF16)
+            for receiver in range(everyone.shape[0]):
+                everyone[receiver, rows, columns] = scaled
+    count = tokens.shape[0]
+    named = routes[...] == 0
+    chances = probs[...].astype(F32)
+    first, second = named[0:1, :], named[1:2, :]
+    chosen = jnp.where(jnp.logical_or(first, second), 1.0, 0.0)
+    weight = jnp.where(first, chances[0:1, :], jnp.where(second, chances[1:2, :], 0.0))
+    down = lax.broadcasted_iota(jnp.int32, (count, count), 0)
+    across = lax.broadcasted_iota(jnp.int32, (count, count), 1)
+
+    def column(mask, row):
+        return jnp.sum(jnp.where(mask, row, 0.0), axis=1, keepdims=True)
+
+    chosen_column = column(down == across, chosen)
+    weight_column = column(down == across, weight)
+    place_column = column(across <= down, chosen)
+    wide_weight = jnp.broadcast_to(weight_column, (count, 128))
+    parts = (tokens[...].astype(F32), out_grad[...].astype(F32), wide_weight)
+    starts = (0, width, 2 * width)
+    for start, part in zip(starts, parts):
+        picked = []
+        for slot in range(CAP):
+            here = jnp.where(place_column == slot + 1.0, chosen_column, 0.0)
+            picked.append(jnp.sum(here * part, axis=0, keepdims=True))
+        block = jnp.concatenate(picked, axis=0).astype(BF16)
+        payload[:, start : start + part.shape[1]] = block
 
 
 def local(
@@ -33,35 +85,32 @@
     down_scales,
 ):
     width = tokens.shape[1]
-    first = routes[:, 0] == 0
-    second = routes[:, 1] == 0
-    chosen = jnp.logical_or(first, second)
-    weight = jnp.where(
-        first, probs[:, 0], jnp.where(second, probs[:, 1], jnp.zeros_like(probs[:, 0]))
-    )
-    slot = jnp.cumsum(chosen.astype(jnp.int32)) - 1
-    slot_ids = jnp.arange(CAP, dtype=jnp.int32)
-    select_mask = jnp.logical_and(slot[None, :] == slot_ids[:, None], chosen[None, :])
-    select = select_mask.astype(BF16)
-    wide_weight = jnp.broadcast_to(weight[:, None], (weight.shape[0], 128))
-    both = jnp.concatenate([tokens, out_grad, wide_weight], axis=1)
-    payload = jnp.dot(select, both, preferred_element_type=F32).astype(BF16)
-
-    own = jnp.concatenate(
-        [
-            dequantize(gate_elems, gate_scales),
-            dequantize(up_elems, up_scales),
-            dequantize(down_elems.T, down_scales.T),
-        ],
-        axis=1,
-    )
-    everyone = jnp.broadcast_to(own[None], (N_FSDP,) + own.shape)
-    everyone, payload = lax.optimization_barrier((everyone, payload))
+    units = gate_elems.shape[1]
+    own_shape = (gate_elems.shape[0], 3 * units)
+    payload, everyone = pl.pallas_call(
+        prepare,
+        out_shape=(
+            jax.ShapeDtypeStruct((CAP, 2 * width + 128), BF16),
+            jax.ShapeDtypeStruct((N_FSDP,) + own_shape, BF16),
+        ),
+        compiler_params=pltpu.CompilerParams(vmem_limit_bytes=60 * 1024 * 1024),
+    )(
+        tokens,
+        out_grad,
+        routes.T,
+        probs.T,
+        gate_elems,
+        gate_scales,
+        up_elems,
+        up_scales,
+        down_elems.T,
+        down_scales.T,
+    )
     weights = lax.all_to_all(everyone, ("x", "y"), 0, 0, tiled=True)
 
-    along_z = lax.all_gather(payload[None], FAR_AXES, axis=0, tiled=True)
-    along_z = along_z.reshape(FAR * CAP, payload.shape[1])
-    along_z = lax.all_gather(along_z, NEAR_AXES, axis=0, tiled=True)
+    along_z = lax.all_gather(payload[None], ("za", "zb", "zc"), axis=0, tiled=True)
+    along_z = along_z.reshape(2 * FAR * CAP, payload.shape[1])
+    along_z = lax.all_gather(along_z, "zd", axis=0, tiled=True)
     along_z, weights = lax.optimization_barrier((along_z, weights))
     pair = jnp.broadcast_to(along_z[None], (CORES,) + along_z.shape)
     pair = lax.all_to_all(pair, "core", 0, 0, tiled=True)
@@ -70,8 +119,7 @@
     grads_rows = all_rows[:, width : 2 * width]
     row_weights = all_rows[:, 2 * width : 2 * width + 1].astype(F32)
 
-    weights = weights.reshape(N_FSDP * own.shape[0], own.shape[1])
-    units = gate_elems.shape[1]
+    weights = weights.reshape(N_FSDP * own_shape[0], own_shape[1])
     w_gate, w_up, w_down = (
         weights[:, :units],
         weights[:, units : 2 * units],
@@ -103,7 +151,7 @@
         ],
         axis=1,
     ).astype(BF16)
-    terms = terms.reshape((N_FSDP,) + own.shape)
+    terms = terms.reshape((N_FSDP,) + own_shape)
     input_part = lax.dot_general(
         jnp.concatenate([gate_pre_grad, lift_grad], axis=1),
         weights[:, : 2 * units],
@@ -124,7 +172,8 @@
 
     part = pack(input_part, prob_part).reshape(CORES, FAR * NEAR * CAP, -1)
     part = lax.all_to_all(part, "core", 0, 0, tiled=True)
-    part = pack(*unpack(part)).reshape(NEAR, FAR * CAP, -1)
+    part = pack(*unpack(part)).reshape(2, FAR, 2, CAP, -1)
+    part = part.transpose(2, 0, 1, 3, 4).reshape(NEAR, FAR * CAP, -1)
     part = lax.all_to_all(part, NEAR_AXES, 0, 0, tiled=True)
     part = pack(*unpack(part))
     part, terms = lax.optimization_barrier((part, terms))
@@ -142,6 +191,10 @@
     mine = CAP * lax.axis_index("za")
     input_rows, prob_rows = unpack(lax.dynamic_slice_in_dim(part, mine, CAP, axis=1))
 
+    chosen = jnp.any(routes == 0, axis=1)
+    slot = jnp.cumsum(chosen.astype(jnp.int32)) - 1
+    slot_ids = jnp.arange(CAP, dtype=jnp.int32)
+    select_mask = jnp.logical_and(slot[None, :] == slot_ids[:, None], chosen[None, :])
     mask_float = select_mask.astype(F32)
     input_grad = jnp.sum(
         mask_float[:, :, None] * input_rows.astype(BF16).astype(F32)[:, None, :], axis=0

time: 170 us -> 155 us (0.912)
  the two profiles are of different devices: /device:TPU:14 before, /device:TPU:4 now
where the time goes in v3:
time: 155 us
  blocking collectives  87.2 us (56%)
  starting transfers between devices  32.9 us (21%)
  waiting for transfers between devices  15.7 us (10%)
  local copies, waits for them, and re-layouts  6.2 us (4%)
  matrix products  4.55 us (3%)
  other arithmetic  4.38 us (3%)
  Pallas kernels  2.69 us (2%)
    all_gather x1, blocking collectives, local(): lax.all_gather(payload[None], ('za', 'zb', 'zc'), axis=0, tiled=True)  40.3 us
    all_gather x1, blocking collectives, local(): part = lax.all_gather(part[None], 'za', axis=0, tiled=True)  28.7 us
    all_to_all x1, starting transfers between devices, local(): weights = lax.all_to_all(everyone, ('x', 'y'), 0, 0, tiled=True)  16.8 us
    all_to_all x1, waiting for transfers between devices, local(): part = lax.all_to_all(part, NEAR_AXES, 0, 0, tiled=True)  9.37 us
    all_to_all x1, starting transfers between devices, local(): shares = lax.all_to_all(terms, ('x', 'y'), 0, 0, tiled=True)  8.77 us
    all_gather x1, blocking collectives, local(): along_z = lax.all_gather(along_z, 'zd', axis=0, tiled=True)  8.74 us
    ppermute x1, waiting for transfers between devices, halve(): return pack(*unpack(jnp.stack([keep, lax.ppermute(give, axis, SWAP)])))  6.35 us
    all_to_all x1, blocking collectives, local(): pair = lax.all_to_all(pair, 'core', 0, 0, tiled=True)  5.14 us
  transfers between devices with their start and end apart: 4, of which 2 were waited for; matrix products, arithmetic and copies ran while one was open for 4% of the time, Pallas kernels for 0%

profile of v3, /device:TPU:4, one launch (start us, length us, event | category | flops | bytes accessed | tf_op | source)
XLA Modules:
  0.0 154.6 jit_solution(13051753401621868860)
XLA Ops:
  0.6 2.7 %shard_map.137 = (bf16[2,6272]{1,0:T(2,128)(2,1)}, bf16[16,192,384]{2,1,0:T(8,128)(2,1)}) custom-call(bf16[8,3072]{1,0:T(8,128)(2,1)} %tokens.1, bf16[8,3072]{1,0:T(8,128)(2,1)} %out_grad.1, s32[2,8]{1,0:T(2,128)} %bitcast.45, bf16[2,8]{1,0:T(2,128)(2,1)} %bitcast.46, bf16[192,128]{1,0:T(8,128)(2,1)} %gate_elems.1, bf16[6,128]{1,0:T(8,128)(2,1)} %gate_scales.1, ...), custom_call_target="tpu_custom_call" | custom-call | tf_op jit(solution)/shard_map/pallas_call | solution.py:90
  3.3 16.8 %all-to-all-start = ((bf16[16,192,384]{2,1,0:T(8,128)(2,1)}), bf16[16,192,384]{2,1,0:T(8,128)(2,1)S(1)}, u32[]{:S(2)}, u32[]{:S(2)}) async-start(bf16[16,192,384]{2,1,0:T(8,128)(2,1)} %get-tuple-element.12), calls=%async_computation | async-start | bytes 4718592 | tf_op jit(solution)/shard_map/all_to_all | solution.py:109
  20.2 40.3 %all-gather.1 = bf16[16,2,6272]{2,1,0:T(2,128)(2,1)S(1)} all-gather(bf16[1,2,6272]{2,1,0:T(2,128)(2,1)S(1)} %bitcast.43), channel_id=2, replica_groups=mesh['za'=4,'zb'=2,'zc'=2,'zd'=2,'core'=2,'x'=4,'y'=4] {'za','zb','zc'}, dimensions={0}, use_global_device_ids=true | all-gather | bytes 426496 | tf_op jit(solution)/shard_map/all_gather | solution.py:111
  60.4 0.9 reshape.153
  61.3 8.7 %all_gather.10 = bf16[64,6272]{1,0:T(8,128)(2,1)S(1)} all-gather(bf16[32,6272]{1,0:T(8,128)(2,1)} %reshape.153), channel_id=1, replica_groups=mesh['za'=4,'zb'=2,'zc'=2,'zd'=2,'core'=2,'x'=4,'y'=4] {'zd'}, dimensions={0}, use_global_device_ids=true | all-gather | bytes 1204224 | tf_op jit(solution)/shard_map/all_gather | solution.py:113
  70.1 1.4 copy-done
  71.6 5.1 %all_to_all.25 = bf16[2,64,6272]{2,1,0:T(8,128)(2,1)S(1)} all-to-all(bf16[2,64,6272]{2,1,0:T(8,128)(2,1)S(1)} %broadcast_in_dim.13), channel_id=1, replica_groups=mesh['za'=4,'zb'=2,'zc'=2,'zd'=2,'core'=2,'x'=4,'y'=4] {'core'}, dimensions={0} | all-to-all | bytes 3211264 | tf_op jit(solution)/shard_map/all_to_all | solution.py:116
  76.8 0.4 fusion.3
  77.2 0.4 fusion.1
  77.7 0.4 multiply_reduce_fusion.1
  78.5 2.1 %convolution_convert_fusion.3 = bf16[128,3072]{1,0:T(8,128)(2,1)S(1)} fusion(bf16[3072,384]{1,0:T(8,128)(2,1)} %bitcast.32, bf16[128,128]{0,1:T(8,128)(2,1)S(1)} %get-tuple-element.30, bf16[128,128]{0,1:T(8,128)(2,1)S(1)} %get-tuple-element.29), kind=kOutput, calls=%fused_computation.4 | convolution fusion | flops 201850880 | bytes 2424832 | tf_op jit(solution)/shard_map/dot_general | solution.py:155
  80.9 4.4 %all_to_all.26 = bf16[2,64,3200]{2,1,0:T(8,128)(2,1)S(1)} all-to-all(bf16[2,64,3200]{2,1,0:T(8,128)(2,1)S(1)} %concatenate.31), channel_id=1, replica_groups=mesh['za'=4,'zb'=2,'zc'=2,'zd'=2,'core'=2,'x'=4,'y'=4] {'core'}, dimensions={0} | all-to-all | bytes 1638400 | tf_op jit(solution)/shard_map/all_to_all | solution.py:174
  86.5 0.9 reshape.146
  87.4 3.5 %all-to-all-start.3 = ((bf16[4,16,3200]{2,1,0:T(8,128)(2,1)}), bf16[4,16,3200]{2,1,0:T(8,128)(2,1)S(1)}, u32[]{:S(2)}, u32[]{:S(2)}) async-start(bf16[4,16,3200]{2,1,0:T(8,128)(2,1)} %reshape.146), calls=%async_computation.3 | async-start | bytes 819200 | tf_op jit(solution)/shard_map/all_to_all | solution.py:177
  91.5 0.4 convolution_convert_fusion.2
  92.3 1.8 %pad_maximum_fusion = bf16[16,192,384]{2,1,0:T(8,128)(2,1)} fusion(bf16[16,192,128]{2,1,0:T(8,128)(2,1)S(1)} %bitcast.38, bf16[16,192,128]{2,1,0:T(8,128)(2,1)S(1)} %bitcast.36, bf16[16,192,128]{2,1,0:T(8,128)(2,1)S(1)} %bitcast.37), kind=kLoop, calls=%fused_computation.5 | loop fusion | flops 7077888 | bytes 4718592 | tf_op jit(solution)/shard_map/concatenate | solution.py:146
  94.1 9.4 %all-to-all-done.3 = bf16[4,16,3200]{2,1,0:T(8,128)(2,1)S(1)} async-done(((bf16[4,16,3200]{2,1,0:T(8,128)(2,1)}), bf16[4,16,3200]{2,1,0:T(8,128)(2,1)S(1)}, u32[]{:S(2)}, u32[]{:S(2)}) %all-to-all-start.3) | async-done | bytes 409632 | tf_op jit(solution)/shard_map/all_to_all | solution.py:177
  103.7 8.8 %all-to-all-start.4 = ((bf16[16,192,384]{2,1,0:T(8,128)(2,1)}), bf16[16,192,384]{2,1,0:T(8,128)(2,1)S(1)}, u32[]{:S(2)}, u32[]{:S(2)}) async-start(bf16[16,192,384]{2,1,0:T(8,128)(2,1)} %pad_maximum_fusion), calls=%async_computation.4 | async-start | bytes 4718592 | tf_op jit(solution)/shard_map/all_to_all | solution.py:180
  112.7 3.8 %collective-permute-start = (bf16[4,2,3200]{2,0,1:T(4,128)(2,1)S(1)}, bf16[4,2,3200]{2,0,1:T(4,128)(2,1)S(1)}, u32[]{:S(2)}, u32[]{:S(2)}) collective-permute-start(bf16[4,2,3200]{2,0,1:T(4,128)(2,1)S(1)} %copy.62), channel_id=1, source_target_pairs={{0,128},{128,0},{1,129},{129,1},{2,130},{130,2},{3,131},{131,3},{4... | collective-permute-start | bytes 153608 | tf_op jit(solution)/shard_map/ppermute | solution.py:187
  116.6 6.3 %collective-permute-done = bf16[4,2,3200]{2,0,1:T(4,128)(2,1)S(1)} collective-permute-done((bf16[4,2,3200]{2,0,1:T(4,128)(2,1)S(1)}, bf16[4,2,3200]{2,0,1:T(4,128)(2,1)S(1)}, u32[]{:S(2)}, u32[]{:S(2)}) %collective-permute-start) | collective-permute-done | bytes 51232 | tf_op jit(solution)/shard_map/ppermute | solution.py:187
  123.2 28.7 %all_gather.11 = bf16[4,8,3200]{2,1,0:T(8,128)(2,1)S(1)} all-gather(bf16[1,8,3200]{2,1,0:T(8,128)(2,1)S(1)} %broadcast_in_dim_reshape.3), channel_id=1, replica_groups=mesh['za'=4,'zb'=2,'zc'=2,'zd'=2,'core'=2,'x'=4,'y'=4] {'za'}, dimensions={0}, use_global_device_ids=true | all-gather | bytes 256000 | tf_op jit(solution)/shard_map/all_gather | solution.py:190
  152.3 0.6 select_reduce_fusion
  152.9 0.7 multiply_reduce_fusion
  153.9 0.7 slice_bitcast_fusion
  (56 shorter events, 4.4 us)
Async XLA Ops:
  3.3 16.9 %copy-start.2 = (bf16[2,6272]{1,0:T(2,128)(2,1)S(1)}, bf16[2,6272]{1,0:T(2,128)(2,1)}, u32[]{:S(2)}) copy-start(bf16[2,6272]{1,0:T(2,128)(2,1)} %get-tuple-element.11) | copy-start | bytes 75268
  3.3 66.8 %all-to-all-start = ((bf16[16,192,384]{2,1,0:T(8,128)(2,1)}), bf16[16,192,384]{2,1,0:T(8,128)(2,1)S(1)}, u32[]{:S(2)}, u32[]{:S(2)}) async-start(bf16[16,192,384]{2,1,0:T(8,128)(2,1)} %get-tuple-element.12), calls=%async_computation | async-start | bytes 4718592 | tf_op jit(solution)/shard_map/all_to_all | solution.py:109
  70.1 1.4 copy-start
  71.6 5.1 %copy-start.1 = (bf16[16,192,384]{2,1,0:T(8,128)(2,1)S(1)}, bf16[16,192,384]{2,1,0:T(8,128)(2,1)}, u32[]{:S(2)}) copy-start(bf16[16,192,384]{2,1,0:T(8,128)(2,1)} %copy-done) | copy-start | bytes 7077892
  85.5 5.4 %copy-start.3 = (s32[8,2]{0,1:T(2,128)S(1)}, s32[8,2]{0,1:T(2,128)}, u32[]{:S(2)}) copy-start(s32[8,2]{0,1:T(2,128)} %param.12) | copy-start | bytes 196
  87.4 16.0 %all-to-all-start.3 = ((bf16[4,16,3200]{2,1,0:T(8,128)(2,1)}), bf16[4,16,3200]{2,1,0:T(8,128)(2,1)S(1)}, u32[]{:S(2)}, u32[]{:S(2)}) async-start(bf16[4,16,3200]{2,1,0:T(8,128)(2,1)} %reshape.146), calls=%async_computation.3 | async-start | bytes 819200 | tf_op jit(solution)/shard_map/all_to_all | solution.py:177
  103.7 49.9 %all-to-all-start.4 = ((bf16[16,192,384]{2,1,0:T(8,128)(2,1)}), bf16[16,192,384]{2,1,0:T(8,128)(2,1)S(1)}, u32[]{:S(2)}, u32[]{:S(2)}) async-start(bf16[16,192,384]{2,1,0:T(8,128)(2,1)} %pad_maximum_fusion), calls=%async_computation.4 | async-start | bytes 4718592 | tf_op jit(solution)/shard_map/all_to_all | solution.py:180
  112.7 10.2 %collective-permute-start = (bf16[4,2,3200]{2,0,1:T(4,128)(2,1)S(1)}, bf16[4,2,3200]{2,0,1:T(4,128)(2,1)S(1)}, u32[]{:S(2)}, u32[]{:S(2)}) collective-permute-start(bf16[4,2,3200]{2,0,1:T(4,128)(2,1)S(1)} %copy.62), channel_id=1, source_target_pairs={{0,128},{128,0},{1,129},{129,1},{2,130},{130,2},{3,131},{131,3},{4... | collective-permute-start | bytes 153608 | tf_op jit(solution)/shard_map/ppermute | solution.py:187
